TPU v7x, 512 devices: a whole 4x4x16 slice. The times are simulated.
512 devices in a mesh: row: 32 (over z, x_hi), col: 16 (over y, x_lo, core).
Axes of the slice: x: 4 (x_hi: 2, x_lo: 2; x = x_hi * 2 + x_lo), y: 4, z: 16, core: 2. Of those that a mesh axis runs over, the one named last changes fastest.
Arguments:
- merged_vectors: float32 [512, 102400], P('col', 'row'), may hold values from -6 to 6
- deflation: int32 [512], replicated, may hold values from 0 to 511, as said below
- vectors: float32 [4, 102400, 256], P(None, ('row', 'col')), may hold values from -0.0390625 to 0.0390625
- factors: float32 [4, 256, 256], replicated, may hold values from -0.25 to 2, as said below
Outputs:
- eigenvectors: float32 [512, 102400], P('col', 'row')
Inputs may be any that keep to these rules, and one draw needn't show every extreme that they name: deflation is a permutation of the 512 eigenvectors; of the 32 eigenvectors held by one index of col, at most 4 are bound for any one index of col, and in every draw every index of col receives exactly 4 from some index. Each factors[b] is upper triangular.
All inputs are finite; a program needn't handle non-finite values.
Results may differ from a plain program's by a relative error of at most 0.0003.
Values sent between devices are 32-bit elements; how exact they have to be, the bound alone decides.
A program may use at most 128 MiB of HBM per device.

v0:
```python
import jax
import jax.numpy as jnp
from jax import lax
from jax.sharding import PartitionSpec as P

contract_plain = (((1,), (0,)), ((), ()))
contract_right = (((1,), (1,)), ((), ()))


def split_parts(values):
    upper = lax.optimization_barrier(values.astype(jnp.bfloat16))
    lower = (values - upper.astype(jnp.float32)).astype(jnp.bfloat16)
    return (upper, lower)


def plain_dot(first_arg, second_arg, numbers):
    return lax.dot_general(first_arg, second_arg, numbers, preferred_element_type=jnp.float32)


def split_dot(first_parts, second_parts, numbers):
    total = plain_dot(first_parts[0], second_parts[0], numbers)
    total = total + plain_dot(first_parts[0], second_parts[1], numbers)
    return total + plain_dot(first_parts[1], second_parts[0], numbers)


def exact_dot(first_arg, second_arg, numbers):
    return lax.dot_general(
        first_arg,
        second_arg,
        numbers,
        precision=lax.Precision.HIGHEST,
        preferred_element_type=jnp.float32,
    )


def deflate(held, deflation):
    members = lax.axis_size("col")
    own_index = lax.axis_index("col")
    own_rows = held.shape[0]
    capacity = 2 * own_rows // members
    sources_table = deflation.reshape(members, own_rows)
    source_dev = sources_table // own_rows
    source_row = sources_table % own_rows
    outbound = source_dev == own_index
    ranking = jnp.cumsum(outbound.astype(jnp.int32), axis=1) - 1
    slot_ids = jnp.arange(capacity, dtype=jnp.int32)
    selected = outbound[:, None, :] & (ranking[:, None, :] == slot_ids[None, :, None])
    picked = jnp.sum(jnp.where(selected, source_row[:, None, :], 0), axis=2)
    filled = jnp.any(selected, axis=2)
    outgoing = jnp.where(filled[:, :, None], held[picked], jnp.float32(0.0))
    incoming = lax.all_to_all(outgoing, "col", split_axis=0, concat_axis=0, tiled=True)
    anchor = lax.dynamic_index_in_dim(source_dev, own_index, 0, keepdims=False)
    slot_index = jnp.arange(own_rows, dtype=jnp.int32)
    same_source = anchor[:, None] == anchor[None, :]
    earlier = slot_index[:, None] > slot_index[None, :]
    position = jnp.sum((same_source & earlier).astype(jnp.int32), axis=1)
    flat = incoming.reshape(members * capacity, incoming.shape[2])
    return flat[anchor * capacity + position]


def apply_block(current, vector_parts, factor, projected):
    combined = exact_dot(projected, factor, contract_right)
    return current - split_dot(split_parts(combined), vector_parts, contract_right)


def per_device(merged_vectors, deflation, vectors, factors):
    arranged = deflate(merged_vectors, deflation)
    block_count = vectors.shape[0]
    gathered = lax.all_gather(vectors, "col", axis=1, tiled=True)
    current = arranged
    for block_id in range(block_count - 1, -1, -1):
        vector_parts = split_parts(gathered[block_id])
        partial_sum = split_dot(split_parts(current), vector_parts, contract_plain)
        projected = lax.psum(partial_sum, "row")
        current = apply_block(current, vector_parts, factors[block_id], projected)
    return current


def solution(mesh):
    in_specs = (P("col", "row"), P(), P(None, ("row", "col"), None), P())
    out_specs = P("col", "row")
    return jax.shard_map(
        per_device, mesh=mesh, in_specs=in_specs, out_specs=out_specs, check_vma=False
    )
```

profile of v0, /device:TPU:8, one launch (start us, length us, event | category | flops | bytes accessed | tf_op | source)
XLA Modules:
  0.0 728.4 jit_solution(2316245301037401851)
XLA Ops:
  6.5 0.7 all-gather.2.cloned.1.call-update
  7.3 0.8 reshape.136
  8.9 0.9 gather_fusion
  10.0 1.2 broadcast_select_fusion
  11.2 9.2 %all-to-all-start = ((f32[16,4,3200]{2,1,0:T(4,128)}), f32[16,4,3200]{2,1,0:T(4,128)S(1)}, u32[]{:S(2)}, u32[]{:S(2)}) async-start(f32[16,4,3200]{2,1,0:T(4,128)} %broadcast_select_fusion), calls=%async_computation | async-start | bytes 1638400 | tf_op jit(solution)/shard_map/all_to_all | solution.py:51
  20.6 11.3 %all-to-all-done = f32[16,4,3200]{2,1,0:T(4,128)S(1)} async-done(((f32[16,4,3200]{2,1,0:T(4,128)}), f32[16,4,3200]{2,1,0:T(4,128)S(1)}, u32[]{:S(2)}, u32[]{:S(2)}) %all-to-all-start) | async-done | bytes 819232 | tf_op jit(solution)/shard_map/all_to_all | solution.py:51
  32.2 0.7 gather_fusion.1
  33.0 62.9 %all-gather.2.cloned.1.call-done = f32[4,3200,256]{2,1,0:T(8,128)} async-done(((f32[4,200,256]{2,1,0:T(8,128)}), f32[4,3200,256]{2,1,0:T(8,128)}) %all-gather.2.cloned.1.call-update) | async-done | bytes 13107216 | tf_op jit(solution)/shard_map/all_gather | solution.py:69
  95.9 7.1 fusion.7
  103.3 2.5 convolution_add_fusion.15
  106.2 149.9 %psum.28 = f32[32,256]{1,0:T(8,128)S(1)} all-reduce(f32[32,256]{1,0:T(8,128)S(1)} %convolution_add_fusion.14), channel_id=1, replica_groups=mesh['row'=32,'col'=16] {'row'}, use_global_device_ids=true, to_apply=%region_4.5 | all-reduce | flops 8192 | bytes 65536 | tf_op jit(solution)/shard_map/psum | solution.py:74
  256.1 1.4 fusion.28
  257.5 2.0 fusion.36
  259.5 2.6 convolution_add_fusion.7
  262.1 0.6 fusion.29
  262.8 0.8 copy-done.3
  263.9 2.4 convolution_add_fusion.13
  266.7 142.4 %psum.29 = f32[32,256]{1,0:T(8,128)S(1)} all-reduce(f32[32,256]{1,0:T(8,128)S(1)} %convolution_add_fusion.12), channel_id=1, replica_groups=mesh['row'=32,'col'=16] {'row'}, use_global_device_ids=true, to_apply=%region_5.6 | all-reduce | flops 8192 | bytes 65536 | tf_op jit(solution)/shard_map/psum | solution.py:74
  409.1 1.4 fusion.30
  410.5 2.0 fusion.38
  412.5 2.6 convolution_add_fusion.5
  415.8 0.8 copy-done.1
  417.0 2.4 convolution_add_fusion.11
  419.7 143.9 %psum.30 = f32[32,256]{1,0:T(8,128)S(1)} all-reduce(f32[32,256]{1,0:T(8,128)S(1)} %convolution_add_fusion.10), channel_id=1, replica_groups=mesh['row'=32,'col'=16] {'row'}, use_global_device_ids=true, to_apply=%region_6.7 | all-reduce | flops 8192 | bytes 65536 | tf_op jit(solution)/shard_map/psum | solution.py:74
  563.6 1.4 fusion.32
  565.0 2.0 fusion.40
  567.1 2.6 convolution_add_fusion.3
  570.7 2.4 convolution_add_fusion.9
  573.4 142.4 %psum.31 = f32[32,256]{1,0:T(8,128)S(1)} all-reduce(f32[32,256]{1,0:T(8,128)S(1)} %convolution_add_fusion.8), channel_id=1, replica_groups=mesh['row'=32,'col'=16] {'row'}, use_global_device_ids=true, to_apply=%region_7.8 | all-reduce | flops 8192 | bytes 65536 | tf_op jit(solution)/shard_map/psum | solution.py:74
  715.8 1.3 fusion.34
  717.7 2.6 convolution_add_fusion.1
  720.2 1.4 fusion.3
  (41 shorter events, 6.2 us)
Async XLA Ops:
  6.5 2.3 copy-start
  6.5 89.3 %all-gather.2.cloned.1.call-start = ((), (), s32[]{:S(2)}) async-start(), calls=%async_computation.1 | async-start | bytes 13926400 | tf_op jit(solution)/shard_map/all_gather | solution.py:69
  11.2 20.8 %all-to-all-start = ((f32[16,4,3200]{2,1,0:T(4,128)}), f32[16,4,3200]{2,1,0:T(4,128)S(1)}, u32[]{:S(2)}, u32[]{:S(2)}) async-start(f32[16,4,3200]{2,1,0:T(4,128)} %broadcast_select_fusion), calls=%async_computation | async-start | bytes 1638400 | tf_op jit(solution)/shard_map/all_to_all | solution.py:51
  103.0 2.9 copy-start.5
  256.1 3.5 copy-start.6
  262.1 1.4 copy-start.3
  409.1 3.5 copy-start.4
  415.1 1.4 copy-start.1
  563.6 3.5 copy-start.2
Sparse Core Ops, SparseCore 0:
  9.5 86.3 all-gather.1
where the time goes:
time: 729 us; the launch traced here: 728 us
  blocking collectives  578 us (79%)
  waiting for transfers between devices  74.9 us (10%)
  matrix products  38.3 us (5%)
  between operations  13.7 us (2%)
  local copies, waits for them, and re-layouts  11.9 us (2%)
  starting transfers between devices  9.25 us (1%)
    psum x4, blocking collectives, per_device(): projected = lax.psum(partial_sum, 'row')  578 us
    all_gather x1, waiting for transfers between devices, per_device(): gathered = lax.all_gather(vectors, 'col', axis=1, tiled=True)  62.9 us
    dot_general x24, matrix products, plain_dot(): lax.dot_general(first_arg, second_arg, numbers, preferred_element_type=jn...  32.8 us
  transfers between devices with their start and end apart: 2, of which 2 were waited for; matrix products, arithmetic and copies ran while one was open for 1% of the time, Pallas kernels for 0%

commit v1 on v0

v1 whole, which is shorter than its diff:
```python
import jax
import jax.numpy as jnp
from jax import lax
from jax.experimental import pallas as pl
from jax.experimental.pallas import tpu as pltpu
from jax.sharding import PartitionSpec as P

MESH = pl.DeviceIdType.MESH
F32, BF16 = jnp.float32, jnp.bfloat16
YN, XN, ZN = 4, 4, 16
NB = 256
BLOCKS = 4
ROWS = 32
SHARD = 200
PAIRS = 3
PLAIN = (((1,), (0,)), ((), ()))
RIGHT = (((1,), (1,)), ((), ()))
LEFT = (((0,), (0,)), ((), ()))


def split_parts(values):
    upper = values.astype(BF16)
    return upper, (values - upper.astype(F32)).astype(BF16)


def dot(a, b, numbers):
    return lax.dot_general(a, b, numbers, preferred_element_type=F32)


def split_dot(a, b, numbers):
    return dot(a[0], b[0], numbers) + dot(a[0], b[1], numbers) + dot(a[1], b[0], numbers)


def device(z, x, y, core):
    return (z * 2 + x // 2, y * 4 + (x % 2) * 2 + core)


def send(src, dst, sems, index, where):
    copy = pltpu.make_async_remote_copy(
        src_ref=src,
        dst_ref=dst,
        send_sem=sems.at[0, index],
        recv_sem=sems.at[1, index],
        device_id=where,
        device_id_type=MESH,
    )
    copy.start()
    return copy


def padded(values):
    return jnp.concatenate([values, jnp.zeros((NB - SHARD, values.shape[1]), F32)], axis=0)


def kernel(
    order_ref, a_ref, v_ref, f_ref, out_ref,
    v_other, v_up, v_low, f_up, f_low,
    a_send, a_recv,
    p_part, p_y, p_x_in, p_x, p_z_in, p_z, p_z_own, p_sum,
    g_part, g_y, g_x_in, g_x, g_z_in, g_z, g_z_own, g_sum, g_all,
    w_all, o_part, o_both, o_send, o_recv,
    v_sems, a_sems, py_sems, px_sems, pz_sems, pg_sems,
    gy_sems, gx_sems, gz_sems, gg_sems, gxa_sems, gya_sems, gc_sems,
    wx_sems, wy_sems, oc_sems, o_sems,
):
    row = lax.axis_index("row")
    col = lax.axis_index("col")
    z, y, core = row // 2, col // 4, col % 2
    x_low = (col // 2) % 2
    x = (row % 2) * 2 + x_low
    chip = y * 2 + x_low
    sent = []

    y_peers = [(d, device(z, x, (y + d) % YN, core)) for d in range(1, YN)]
    x_peers = [(d, device(z, (x + d) % XN, y, core)) for d in range(1, XN)]
    z_peers = [(d, device((z + d) % ZN, x, y, core)) for d in range(1, ZN)]
    group = []
    for dy in range(YN):
        for dx in range(2):
            for dc in range(2):
                group.append(((y + dy) % YN, (x_low + dx) % 2, (core + dc) % 2))
    col_peers = [(row, gy * 4 + gx * 2 + gc) for gy, gx, gc in group[1:]]
    far_x = [device(z, (x // 2 * 2 + 2) % XN + h, y, core) for h in range(2)]
    other_core = (row, y * 4 + x_low * 2 + 1 - core)

    barrier = pltpu.get_barrier_semaphore()
    peers = col_peers + far_x + [peer for _, peer in z_peers]
    for peer in peers:
        pl.semaphore_signal(barrier, inc=1, device_id=peer, device_id_type=MESH)

    a_value = a_ref[...]
    gap = jnp.zeros((ROWS, NB - SHARD), F32)
    for s in range(8):
        first = a_value[:, s * 400 : s * 400 + 200]
        second = a_value[:, s * 400 + 200 : s * 400 + 400]
        a_send[s] = jnp.concatenate([first, gap, second, gap], axis=1)
    a_recv[chip] = a_send[chip]
    for b in range(BLOCKS):
        up, low = split_parts(padded(v_ref[b]))
        v_up[b, core] = up
        v_low[b, core] = low
        up, low = split_parts(f_ref[b])
        f_up[b] = up
        f_low[b] = low

    pl.semaphore_wait(barrier, len(peers))

    v_copy = send(v_ref, v_other, v_sems, 0, other_core)
    sent.append(v_copy)
    a_copies = []
    for i, (gy, gx, gc) in enumerate(group[2::2]):
        a_copies.append(
            send(a_send.at[gy * 2 + gx], a_recv.at[chip], a_sems, i, (row, gy * 4 + gx * 2 + core))
        )
    sent += a_copies

    v_copy.wait_recv()
    for b in range(BLOCKS):
        up, low = split_parts(padded(v_other[b]))
        v_up[b, 1 - core] = up
        v_low[b, 1 - core] = low

    def v_parts(b):
        return v_up[b].reshape(2 * NB, NB), v_low[b].reshape(2 * NB, NB)

    lefts = (3, 3 - core, 2 - core)
    rights = (2 - 2 * core, 1 - core, 1 - core)
    for j in range(PAIRS):
        g_part[j] = split_dot(v_parts(lefts[j]), v_parts(rights[j]), LEFT)

    def start_y(part, into, sems):
        return [
            send(part.at[:, pl.ds((y + d) % YN * 64, 64), :], into.at[d - 1], sems, d - 1, peer)
            for d, peer in y_peers
        ]

    def finish_y(copies, part, into, total):
        for copy in copies:
            copy.wait_recv()
        total[...] = part[:, pl.ds(y * 64, 64), :] + into[0] + into[1] + into[2]

    def start_x(total, into, sems):
        return [
            send(total.at[:, pl.ds((x + d) % XN * 16, 16), :], into.at[d - 1], sems, d - 1, peer)
            for d, peer in x_peers
        ]

    def finish_x(copies, total, into, tiles, count):
        for copy in copies:
            copy.wait_recv()
        value = total[:, pl.ds(x * 16, 16), :] + into[0] + into[1] + into[2]
        for t in range(ZN):
            j, g, h = t // 4, t // 2 % 2, t % 2
            if j < count:
                tiles[t] = value[j, g * 8 : g * 8 + 8, h * 128 : h * 128 + 128]
            else:
                tiles[t] = jnp.zeros((8, 128), F32)

    def start_z(tiles, into, sems):
        return [
            send(tiles.at[(z + d) % ZN], into.at[d - 1], sems, d - 1, peer) for d, peer in z_peers
        ]

    def finish_z(copies, tiles, into, own):
        for copy in copies:
            copy.wait_recv()
        own[z] = tiles[z] + jnp.sum(into[...], axis=0)

    def start_z_back(own, sems):
        return [send(own.at[z], own.at[z], sems, d - 1, peer) for d, peer in z_peers]

    def finish_z_back(copies, own, count):
        for copy in copies:
            copy.wait_recv()
        blocks = []
        for j in range(count):
            halves = [
                jnp.concatenate([own[j * 4 + g * 2], own[j * 4 + g * 2 + 1]], axis=1) for g in range(2)
            ]
            blocks.append(jnp.concatenate(halves, axis=0))
        return blocks

    gy = start_y(g_part, g_y, gy_sems)
    sent += gy

    for copy in a_copies:
        copy.wait_recv()
    a_parts = split_parts(a_recv[...].reshape(8 * ROWS, 2 * NB))
    for b in range(BLOCKS):
        p_part[b] = split_dot(a_parts, v_parts(b), PLAIN)
    py = start_y(p_part, p_y, py_sems)
    sent += py

    finish_y(gy, g_part, g_y, g_x_in)
    gx = start_x(g_x_in, g_x, gx_sems)
    sent += gx
    finish_x(gx, g_x_in, g_x, g_z_in, PAIRS)
    gz = start_z(g_z_in, g_z, gz_sems)
    sent += gz

    finish_y(py, p_part, p_y, p_x_in)
    px = start_x(p_x_in, p_x, px_sems)
    sent += px
    finish_x(px, p_x_in, p_x, p_z_in, BLOCKS)
    pz = start_z(p_z_in, p_z, pz_sems)
    sent += pz

    finish_z(gz, g_z_in, g_z, g_z_own)
    gg = start_z_back(g_z_own, gg_sems)
    sent += gg
    finish_z(pz, p_z_in, p_z, p_z_own)
    pg = start_z_back(p_z_own, pg_sems)
    sent += pg

    for j, block in enumerate(finish_z_back(gg, g_z_own, PAIRS)):
        g_all[core, y, x, j] = block
    mine = g_all.at[core, y, x]
    gxa = [send(mine, mine, gxa_sems, d - 1, peer) for d, peer in x_peers]
    sent += gxa
    for copy in gxa:
        copy.wait_recv()
    mine = g_all.at[core, y]
    gya = [send(mine, mine, gya_sems, d - 1, peer) for d, peer in y_peers]
    sent += gya
    for copy in gya:
        copy.wait_recv()
    mine = g_all.at[core]
    gc = send(mine, mine, gc_sems, 0, other_core)
    sent.append(gc)

    proj = finish_z_back(pg, p_z_own, BLOCKS)
    gc.wait_recv()

    def g_parts(c, j):
        return split_parts(g_all[c, :, :, j].reshape(NB, NB))

    w = {}
    w[3] = split_dot(split_parts(proj[3]), (f_up[3], f_low[3]), RIGHT)
    w3 = split_parts(w[3])
    p2 = proj[2] - split_dot(w3, g_parts(0, 0), PLAIN)
    w[2] = split_dot(split_parts(p2), (f_up[2], f_low[2]), RIGHT)
    w2 = split_parts(w[2])
    p1 = proj[1] - split_dot(w3, g_parts(0, 1), PLAIN) - split_dot(w2, g_parts(0, 2), PLAIN)
    w[1] = split_dot(split_parts(p1), (f_up[1], f_low[1]), RIGHT)
    w1 = split_parts(w[1])
    p0 = (
        proj[0]
        - split_dot(w3, g_parts(1, 0), PLAIN)
        - split_dot(w2, g_parts(1, 1), PLAIN)
        - split_dot(w1, g_parts(1, 2), PLAIN)
    )
    w[0] = split_dot(split_parts(p0), (f_up[0], f_low[0]), RIGHT)
    for b in range(BLOCKS):
        w_all[y, x, b] = w[b]

    mine = w_all.at[y, x]
    wx = [send(mine, mine, wx_sems, d - 1, peer) for d, peer in x_peers]
    sent += wx
    for copy in wx:
        copy.wait_recv()
    mine = w_all.at[y]
    wy = [send(mine, mine, wy_sems, d - 1, peer) for d, peer in y_peers]
    sent += wy
    for copy in wy:
        copy.wait_recv()

    for half in range(2):
        o_part[half] = a_recv[:, :, half * NB : half * NB + NB].reshape(8 * ROWS, NB)
    for b in range(BLOCKS):
        w_parts = split_parts(w_all[:, :, b].reshape(8 * ROWS, NB))
        for half in range(2):
            o_part[half] -= split_dot(w_parts, (v_up[b, half], v_low[b, half]), RIGHT)

    oc = send(o_part.at[1 - core], o_both.at[core], oc_sems, 0, other_core)
    sent.append(oc)
    o_both[core] = o_part[core]
    oc.wait_recv()

    o_copies = []
    for i, (ty, tx, tc) in enumerate(group[1:] + group[:1]):
        target = ty * 4 + tx * 2 + tc

        @pl.loop(0, ROWS, unroll=8)
        def _(k):
            source = order_ref[target * ROWS + k]
            plane = source // ROWS % 2
            place = source // (2 * ROWS) * ROWS + source % ROWS
            o_send[target, pl.ds(k, 1), :] = o_both[plane, pl.ds(place, 1), :]

        if i < 15:
            o_copies.append(send(o_send.at[target], o_recv.at[col], o_sems, i, (row, target)))
    sent += o_copies
    o_recv[col] = o_send[col]
    for copy in o_copies:
        copy.wait_recv()
    for c in range(16):
        out_ref[:, c * SHARD : c * SHARD + SHARD] = o_recv[c][:, :SHARD]

    for copy in sent:
        copy.wait_send()


def vmem(*shape):
    return pltpu.VMEM(shape, F32)


def half_vmem(*shape):
    return pltpu.VMEM(shape, BF16)


def sems(count):
    return pltpu.SemaphoreType.DMA((2, count))


def per_device(merged_vectors, deflation, vectors, factors):
    rows = 8 * ROWS
    reduce_bufs = lambda n: [
        vmem(n, rows, NB), vmem(YN - 1, n, 64, NB), vmem(n, 64, NB), vmem(XN - 1, n, 16, NB),
        vmem(ZN, 8, 128), vmem(ZN - 1, 8, 128), vmem(ZN, 8, 128), vmem(n, 16, NB),
    ]
    scratch = [
        vmem(BLOCKS, SHARD, NB),
        half_vmem(BLOCKS, 2, NB, NB), half_vmem(BLOCKS, 2, NB, NB),
        half_vmem(BLOCKS, NB, NB), half_vmem(BLOCKS, NB, NB),
        vmem(8, ROWS, 2 * NB), vmem(8, ROWS, 2 * NB),
        *reduce_bufs(BLOCKS),
        *reduce_bufs(PAIRS),
        vmem(2, YN, XN, PAIRS, 16, NB),
        vmem(YN, XN, BLOCKS, 16, NB),
        vmem(2, rows, NB), vmem(2, rows, NB),
        vmem(16, ROWS, NB), vmem(16, ROWS, NB),
        sems(1), sems(7), sems(3), sems(3), sems(15), sems(15),
        sems(3), sems(3), sems(15), sems(15), sems(3), sems(3), sems(1),
        sems(3), sems(3), sems(1), sems(15),
    ]
    in_vmem = pl.BlockSpec(memory_space=pltpu.VMEM)
    return pl.pallas_call(
        kernel,
        out_shape=jax.ShapeDtypeStruct(merged_vectors.shape, F32),
        in_specs=[pl.BlockSpec(memory_space=pltpu.SMEM), in_vmem, in_vmem, in_vmem],
        out_specs=in_vmem,
        scratch_shapes=scratch,
        compiler_params=pltpu.CompilerParams(
            collective_id=0, has_side_effects=True, vmem_limit_bytes=48 * 1024 * 1024
        ),
        name="back_transform",
    )(deflation, merged_vectors, vectors, factors)


def solution(mesh):
    in_specs = (P("col", "row"), P(), P(None, ("row", "col"), None), P())
    out_specs = P("col", "row")
    return jax.shard_map(
        per_device, mesh=mesh, in_specs=in_specs, out_specs=out_specs, check_vma=False
    )
```

time: 729 us -> 116 us (0.16)
  the two profiles are of different devices: /device:TPU:8 before, /device:TPU:1 now
where the time goes in v1:
time: 116 us
  Pallas kernels  111 us (96%)
  local copies, waits for them, and re-layouts  4.8 us (4%)
    pallas_call x1, Pallas kernels, per_device(): pl.pallas_call(kernel, out_shape=jax.ShapeDtypeStruct(merged_vectors.shap...  111 us
    unnamed x9, local copies, waits for them, and re-layouts  4.8 us

profile of v1, /device:TPU:1, one launch (start us, length us, event | category | flops | bytes accessed | tf_op | source)
XLA Modules:
  0.0 115.7 jit_solution(3780738178379284473)
XLA Ops:
  0.0 0.0 copy-start
  0.0 1.2 %copy-done = f32[4,256,256]{2,1,0:T(8,128)S(1)} copy-done((f32[4,256,256]{2,1,0:T(8,128)S(1)}, f32[4,256,256]{2,1,0:T(8,128)}, u32[]{:S(2)}) %copy-start) | copy-done | bytes 1048600
  1.2 0.0 copy-start.1
  1.2 1.1 copy-done.1
  2.4 0.0 copy-start.2
  2.4 1.0 copy-done.2
  3.4 0.0 copy-start.3
  3.4 0.7 copy-done.3
  4.1 110.9 %back_transform.1 = f32[32,3200]{1,0:T(8,128)S(1)} custom-call(s32[512]{0:T(512)S(1)} %copy-done.3, f32[32,3200]{1,0:T(8,128)S(1)} %copy-done.2, f32[4,200,256]{2,1,0:T(8,128)S(1)} %copy-done.1, f32[4,256,256]{2,1,0:T(8,128)S(1)} %copy-done), custom_call_target="tpu_custom_call" | custom-call | tf_op jit(solution)/shard_map/back_transform/pallas_call | solution.py:337
  114.9 0.8 copy.6
Async XLA Ops:
  0.0 1.2 %copy-start = (f32[4,256,256]{2,1,0:T(8,128)S(1)}, f32[4,256,256]{2,1,0:T(8,128)}, u32[]{:S(2)}) copy-start(f32[4,256,256]{2,1,0:T(8,128)} %f_ref.1) | copy-start | bytes 3145732
  1.2 1.1 copy-start.1
  2.4 1.0 copy-start.2
  3.4 0.7 copy-start.3

commit v2 on v1

v2 whole, which is shorter than its diff:
```python
import jax
import jax.numpy as jnp
from jax import lax
from jax.experimental import pallas as pl
from jax.experimental.pallas import tpu as pltpu
from jax.sharding import PartitionSpec as P

MESH = pl.DeviceIdType.MESH
F32, BF16 = jnp.float32, jnp.bfloat16
YN, XN, ZN = 4, 4, 16
NB = 256
BLOCKS = 4
ROWS = 32
SHARD = 200
PAIRS = 3
PLAIN = (((1,), (0,)), ((), ()))
RIGHT = (((1,), (1,)), ((), ()))
LEFT = (((0,), (0,)), ((), ()))


def split_parts(values):
    upper = values.astype(BF16)
    return upper, (values - upper.astype(F32)).astype(BF16)


def dot(a, b, numbers):
    return lax.dot_general(a, b, numbers, preferred_element_type=F32)


def split_dot(a, b, numbers):
    return dot(a[0], b[0], numbers) + dot(a[0], b[1], numbers) + dot(a[1], b[0], numbers)


def device(z, x, y, core):
    return (z * 2 + x // 2, y * 4 + (x % 2) * 2 + core)


def send(src, dst, sems, index, where):
    copy = pltpu.make_async_remote_copy(
        src_ref=src,
        dst_ref=dst,
        send_sem=sems.at[0, index],
        recv_sem=sems.at[1, index],
        device_id=where,
        device_id_type=MESH,
    )
    copy.start()
    return copy


def padded(values):
    return jnp.concatenate([values, jnp.zeros((NB - SHARD, values.shape[1]), F32)], axis=0)


def kernel(
    order_hbm, a_hbm, v_hbm, f_hbm, out_ref,
    order_ref, a_ref, v_ref, f_ref,
    v_other, v_up, v_low, f_up, f_low,
    a_send, a_recv,
    p_part, p_in1, p_mid, p_in2, p_tiles, p_in3, p_own,
    g_part, g_in1, g_mid, g_in2, g_tiles, g_in3, g_own,
    g_all, w_all, o_part, o_both, o_send, o_recv,
    in_sems, v_sems, a_sems, p1_sems, p2_sems, p3_sems, p4_sems,
    g1_sems, g2_sems, g3_sems, g4_sems, g5_sems, g6_sems, g7_sems,
    w1_sems, w2_sems, oc_sems, o_sems,
):
    row = lax.axis_index("row")
    col = lax.axis_index("col")
    z, y, core = row // 2, col // 4, col % 2
    x_low = (col // 2) % 2
    x = (row % 2) * 2 + x_low
    chip = y * 2 + x_low
    sent = []

    y_peers = [(d, (y + d) % YN, device(z, x, (y + d) % YN, core)) for d in (2, 1, 3)]
    x_peers = [(d, (x + d) % XN, device(z, (x + d) % XN, y, core)) for d in (2, 1, 3)]
    far_first = sorted(range(1, ZN), key=lambda d: -min(d, ZN - d))
    z_peers = [(d, (z + d) % ZN, device((z + d) % ZN, x, y, core)) for d in far_first]
    group = []
    for dy in (2, 1, 3, 0):
        for dx in (1, 0):
            for dc in (1, 0):
                group.append(((y + dy) % YN, (x_low + dx) % 2, (core + dc) % 2))
    col_peers = [(row, gy * 4 + gx * 2 + gc) for gy, gx, gc in group[:-1]]
    far_x = [device(z, (x // 2 * 2 + 2) % XN + h, y, core) for h in range(2)]
    other_core = (row, y * 4 + x_low * 2 + 1 - core)

    barrier = pltpu.get_barrier_semaphore()
    peers = col_peers + far_x + [peer for _, _, peer in z_peers]
    for peer in peers:
        pl.semaphore_signal(barrier, inc=1, device_id=peer, device_id_type=MESH)

    inputs = [
        pltpu.make_async_copy(src, dst, in_sems.at[i])
        for i, (src, dst) in enumerate(
            ((a_hbm, a_ref), (v_hbm, v_ref), (f_hbm, f_ref), (order_hbm, order_ref))
        )
    ]
    for copy in inputs:
        copy.start()

    inputs[0].wait()
    a_value = a_ref[...]
    gap = jnp.zeros((ROWS, NB - SHARD), F32)
    for s in range(8):
        first = a_value[:, s * 400 : s * 400 + 200]
        second = a_value[:, s * 400 + 200 : s * 400 + 400]
        a_send[s] = jnp.concatenate([first, gap, second, gap], axis=1)
    a_recv[chip] = a_send[chip]
    inputs[1].wait()
    for b in range(BLOCKS):
        up, low = split_parts(padded(v_ref[b]))
        v_up[b, core] = up
        v_low[b, core] = low
    inputs[2].wait()
    for b in range(BLOCKS):
        up, low = split_parts(f_ref[b])
        f_up[b] = up
        f_low[b] = low
    inputs[3].wait()

    pl.semaphore_wait(barrier, len(peers))
    v_copy = send(v_ref, v_other, v_sems, 0, other_core)
    sent.append(v_copy)
    a_copies = []
    for i, (gy, gx, gc) in enumerate(group[1:-1:2]):
        a_copies.append(
            send(a_send.at[gy * 2 + gx], a_recv.at[chip], a_sems, i, (row, gy * 4 + gx * 2 + core))
        )
    sent += a_copies

    v_copy.wait_recv()
    for b in range(BLOCKS):
        up, low = split_parts(padded(v_other[b]))
        v_up[b, 1 - core] = up
        v_low[b, 1 - core] = low

    def v_parts(b):
        return v_up[b].reshape(2 * NB, NB), v_low[b].reshape(2 * NB, NB)

    def start_first(half, part, into, sems):
        copies = []
        for d, place, peer in (y_peers, x_peers)[half]:
            src = part.at[0, :, place] if half == 0 else part.at[1, :, :, place]
            copies.append(send(src, into.at[half, d - 1], sems, half * 3 + d - 1, peer))
        sent.extend(copies)
        return copies

    def finish_first(half, copies, part, into, mid):
        for copy in copies:
            copy.wait_recv()
        own = part[0, :, y] if half == 0 else part[1, :, :, x]
        mid[half] = own + into[half, 0] + into[half, 1] + into[half, 2]

    def start_second(half, mid, into, sems):
        copies = []
        for d, place, peer in (x_peers, y_peers)[half]:
            src = mid.at[half, :, place]
            copies.append(send(src, into.at[half, d - 1], sems, half * 3 + d - 1, peer))
        sent.extend(copies)
        return copies

    def finish_second(half, copies, mid, into, tiles):
        for copy in copies:
            copy.wait_recv()
        value = mid[half, :, (x, y)[half]] + into[half, 0] + into[half, 1] + into[half, 2]
        count, lanes = value.shape[0], value.shape[2] // 128
        for t in range(count * 2 * lanes):
            j, g, h = t // (2 * lanes), t // lanes % 2, t % lanes
            piece = value[j, g * 8 : g * 8 + 8, h * 128 : h * 128 + 128]
            tiles[half * count * 2 * lanes + t] = piece

    def start_z(tiles, into, sems):
        copies = [
            send(tiles.at[place], into.at[d - 1], sems, d - 1, peer) for d, place, peer in z_peers
        ]
        sent.extend(copies)
        return copies

    def finish_z(copies, tiles, into, own):
        for copy in copies:
            copy.wait_recv()
        own[z] = tiles[z] + jnp.sum(into[...], axis=0)

    def start_z_back(own, sems):
        copies = [send(own.at[z], own.at[z], sems, d - 1, peer) for d, _, peer in z_peers]
        sent.extend(copies)
        return copies

    def finish_z_back(copies, own, count, lanes):
        for copy in copies:
            copy.wait_recv()
        blocks = []
        for j in range(2 * count):
            base = j * 2 * lanes
            halves = [
                jnp.concatenate([own[base + g * lanes + h] for h in range(lanes)], axis=1)
                for g in range(2)
            ]
            blocks.append(jnp.concatenate(halves, axis=0))
        return blocks

    def start_back(half, whole, sems):
        mine = whole.at[half, :, y, x]
        copies = [
            send(mine, mine, sems, half * 3 + d - 1, peer) for d, _, peer in (x_peers, y_peers)[half]
        ]
        sent.extend(copies)
        return copies

    def finish_back(half, whole, copies, sems):
        for copy in copies:
            copy.wait_recv()
        mine = whole.at[0, :, y] if half == 0 else whole.at[1, :, :, x]
        copies = [
            send(mine, mine, sems, half * 3 + d - 1, peer) for d, _, peer in (y_peers, x_peers)[half]
        ]
        sent.extend(copies)
        return copies

    lefts = (3, 3 - core, 2 - core)
    rights = (2 - 2 * core, 1 - core, 1 - core)
    for j in range(PAIRS):
        product = split_dot(v_parts(lefts[j]), v_parts(rights[j]), LEFT)
        for half in range(2):
            lanes = product[:, half * 128 : half * 128 + 128]
            g_part[half, j] = lanes.reshape(YN, XN, 16, 128)
    g1 = [start_first(half, g_part, g_in1, g1_sems) for half in range(2)]

    for copy in a_copies:
        copy.wait_recv()
    a_parts = split_parts(a_recv[...].reshape(8 * ROWS, 2 * NB))
    p1 = []
    for half in range(2):
        for i in range(2):
            product = split_dot(a_parts, v_parts(3 - 2 * half - i), PLAIN)
            p_part[half, i] = product.reshape(YN, XN, 16, NB)
        p1.append(start_first(half, p_part, p_in1, p1_sems))

    g2 = []
    for half in range(2):
        finish_first(half, g1[half], g_part, g_in1, g_mid)
        g2.append(start_second(half, g_mid, g_in2, g2_sems))
    for half in range(2):
        finish_second(half, g2[half], g_mid, g_in2, g_tiles)
    for t in range(12, ZN):
        g_tiles[t] = jnp.zeros((8, 128), F32)
    g3 = start_z(g_tiles, g_in3, g3_sems)

    p2 = []
    for half in range(2):
        finish_first(half, p1[half], p_part, p_in1, p_mid)
        p2.append(start_second(half, p_mid, p_in2, p2_sems))
    for half in range(2):
        finish_second(half, p2[half], p_mid, p_in2, p_tiles)
    p3 = start_z(p_tiles, p_in3, p3_sems)

    finish_z(g3, g_tiles, g_in3, g_own)
    g4 = start_z_back(g_own, g4_sems)
    finish_z(p3, p_tiles, p_in3, p_own)
    p4 = start_z_back(p_own, p4_sems)

    g_mine = g_all.at[core]
    for j, block in enumerate(finish_z_back(g4, g_own, PAIRS, 1)):
        g_all[core, j // PAIRS, j % PAIRS, y, x] = block
    g5 = [start_back(half, g_mine, g5_sems) for half in range(2)]
    g6 = [finish_back(half, g_mine, g5[half], g6_sems) for half in range(2)]
    g7 = []
    for half in range(2):
        where = y if half == 0 else x
        arrived = [(where, None)] + [
            ((where - d) % 4, copy) for d, copy in zip((2, 1, 3), g6[half])
        ]
        for i, (place, copy) in enumerate(arrived):
            if copy is not None:
                copy.wait_recv()
            piece = g_mine.at[0, :, place] if half == 0 else g_mine.at[1, :, :, place]
            g7.append(send(piece, piece, g7_sems, half * 4 + i, other_core))
    sent += g7

    proj = finish_z_back(p4, p_own, 2, 2)
    w = [None] * BLOCKS
    w[0] = split_dot(split_parts(proj[0]), (f_up[3], f_low[3]), RIGHT)
    for copy in g7:
        copy.wait_recv()

    def g_parts(c, j):
        block = jnp.concatenate(
            [g_all[c, half, j].reshape(NB, 128) for half in range(2)], axis=1
        )
        return split_parts(block)

    places = {(0, 1): (0, 0), (0, 2): (0, 1), (1, 2): (0, 2), (0, 3): (1, 0), (1, 3): (1, 1), (2, 3): (1, 2)}
    w_parts = [split_parts(w[0])]
    w_all[0, 0, y, x] = w[0]
    w1 = []
    for i in range(1, BLOCKS):
        value = proj[i]
        for k in range(i):
            value = value - split_dot(w_parts[k], g_parts(*places[k, i]), PLAIN)
        value = split_dot(split_parts(value), (f_up[3 - i], f_low[3 - i]), RIGHT)
        w_parts.append(split_parts(value))
        w_all[i // 2, i % 2, y, x] = value
        if i % 2 == 1:
            w1.append(start_back(i // 2, w_all, w1_sems))
    w2 = [finish_back(half, w_all, w1[half], w2_sems) for half in range(2)]

    for side in range(2):
        o_part[side] = a_recv[:, :, side * NB : side * NB + NB].reshape(8 * ROWS, NB)
    for half in range(2):
        for copy in w2[half]:
            copy.wait_recv()
        for i in range(2):
            b = 3 - 2 * half - i
            parts = split_parts(w_all[half, i].reshape(8 * ROWS, NB))
            for side in range(2):
                o_part[side] -= split_dot(parts, (v_up[b, side], v_low[b, side]), RIGHT)
    oc = send(o_part.at[1 - core], o_both.at[core], oc_sems, 0, other_core)
    sent.append(oc)
    o_both[core] = o_part[core]
    oc.wait_recv()
    o_copies = []
    for i, (ty, tx, tc) in enumerate(group):
        target = ty * 4 + tx * 2 + tc

        @pl.loop(0, ROWS, unroll=8)
        def _(k):
            source = order_ref[target * ROWS + k]
            plane = source // ROWS % 2
            place = source // (2 * ROWS) * ROWS + source % ROWS
            o_send[target, pl.ds(k, 1), :] = o_both[plane, pl.ds(place, 1), :]

        if i < 15:
            o_copies.append(send(o_send.at[target], o_recv.at[col], o_sems, i, (row, target)))
    sent += o_copies
    o_recv[col] = o_send[col]
    for copy in o_copies:
        copy.wait_recv()
    for c in range(16):
        out_ref[:, c * SHARD : c * SHARD + SHARD] = o_recv[c][:, :SHARD]

    for copy in sent:
        copy.wait_send()


def vmem(*shape):
    return pltpu.VMEM(shape, F32)


def half_vmem(*shape):
    return pltpu.VMEM(shape, BF16)


def sems(count):
    return pltpu.SemaphoreType.DMA((2, count))


def reduce_bufs(n, lanes):
    return [
        vmem(2, n, YN, XN, 16, lanes), vmem(2, 3, n, 4, 16, lanes), vmem(2, n, 4, 16, lanes),
        vmem(2, 3, n, 16, lanes), vmem(ZN, 8, 128), vmem(ZN - 1, 8, 128), vmem(ZN, 8, 128),
    ]


def per_device(merged_vectors, deflation, vectors, factors):
    rows = 8 * ROWS
    scratch = [
        pltpu.SMEM(deflation.shape, jnp.int32), vmem(*merged_vectors.shape),
        vmem(*vectors.shape), vmem(*factors.shape),
        vmem(BLOCKS, SHARD, NB),
        half_vmem(BLOCKS, 2, NB, NB), half_vmem(BLOCKS, 2, NB, NB),
        half_vmem(BLOCKS, NB, NB), half_vmem(BLOCKS, NB, NB),
        vmem(8, ROWS, 2 * NB), vmem(8, ROWS, 2 * NB),
        *reduce_bufs(2, NB),
        *reduce_bufs(PAIRS, 128),
        vmem(2, 2, PAIRS, YN, XN, 16, 128),
        vmem(2, 2, YN, XN, 16, NB),
        vmem(2, rows, NB), vmem(2, rows, NB),
        vmem(16, ROWS, NB), vmem(16, ROWS, NB),
        pltpu.SemaphoreType.DMA((4,)),
        sems(1), sems(7), sems(6), sems(6), sems(15), sems(15),
        sems(6), sems(6), sems(15), sems(15), sems(6), sems(6), sems(8),
        sems(6), sems(6), sems(1), sems(15),
    ]
    in_place = pl.BlockSpec(memory_space=pl.ANY)
    return pl.pallas_call(
        kernel,
        out_shape=jax.ShapeDtypeStruct(merged_vectors.shape, F32),
        in_specs=[in_place] * 4,
        out_specs=pl.BlockSpec(memory_space=pltpu.VMEM),
        scratch_shapes=scratch,
        compiler_params=pltpu.CompilerParams(
            collective_id=0, has_side_effects=True, vmem_limit_bytes=56 * 1024 * 1024
        ),
        name="back_transform",
    )(deflation, merged_vectors, vectors, factors)


def solution(mesh):
    in_specs = (P("col", "row"), P(), P(None, ("row", "col"), None), P())
    out_specs = P("col", "row")
    return jax.shard_map(
        per_device, mesh=mesh, in_specs=in_specs, out_specs=out_specs, check_vma=False
    )
```

time: 116 us -> 92.6 us (0.80)
  Pallas kernels: 111 us -> 90.6 us
  local copies, waits for them, and re-layouts: 4.8 us -> 1.78 us
    pallas_call x1, Pallas kernels: 111 us -> 90.6 us  [per_device(): pl.pallas_call(kernel, out_shape=jax.ShapeDtypeStruct(merged_vectors.shap...]
    unnamed x9 -> x1, local copies, waits for them, and re-layouts: 4.8 us -> 1.78 us
where the time goes in v2:
time: 92.6 us; the launch traced here: 92.4 us
  Pallas kernels  90.6 us (98%)
  local copies, waits for them, and re-layouts  1.78 us (2%)
    pallas_call x1, Pallas kernels, per_device(): pl.pallas_call(kernel, out_shape=jax.ShapeDtypeStruct(merged_vectors.shap...  90.6 us

profile of v2, /device:TPU:1, one launch (start us, length us, event | category | flops | bytes accessed | tf_op | source)
XLA Modules:
  0.0 92.4 jit_solution(12391427604052372364)
XLA Ops:
  0.0 90.6 %back_transform.1 = f32[32,3200]{1,0:T(8,128)} custom-call(s32[512]{0:T(512)} %order_hbm.1, f32[32,3200]{1,0:T(8,128)} %a_hbm.1, f32[4,200,256]{2,1,0:T(8,128)} %v_hbm.1, f32[4,256,256]{2,1,0:T(8,128)} %f_hbm.1), custom_call_target="tpu_custom_call" | custom-call | tf_op jit(solution)/shard_map/back_transform/pallas_call | solution.py:386
  90.6 1.8 %copy.6 = f32[32,3200]{1,0:T(8,128)} copy(f32[32,3200]{1,0:T(8,128)} %back_transform.1) | data formatting | bytes 819200

commit v3 on v2

--- a/solution.py
+++ b/solution.py
@@ -12,6 +12,7 @@
 BLOCKS = 4
 ROWS = 32
 SHARD = 200
+HALF = 128
 PAIRS = 3
 PLAIN = (((1,), (0,)), ((), ()))
 RIGHT = (((1,), (1,)), ((), ()))
@@ -49,20 +50,21 @@
 
 
 def padded(values):
-    return jnp.concatenate([values, jnp.zeros((NB - SHARD, values.shape[1]), F32)], axis=0)
+    rows = jnp.concatenate([values, jnp.zeros((NB - SHARD, values.shape[1]), F32)], axis=0)
+    return rows.reshape(2, HALF, values.shape[1])
 
 
 def kernel(
     order_hbm, a_hbm, v_hbm, f_hbm, out_ref,
-    order_ref, a_ref, v_ref, f_ref,
+    order_ref, place_ref, a_ref, v_ref, f_ref,
     v_other, v_up, v_low, f_up, f_low,
     a_send, a_recv,
     p_part, p_in1, p_mid, p_in2, p_tiles, p_in3, p_own,
     g_part, g_in1, g_mid, g_in2, g_tiles, g_in3, g_own,
-    g_all, w_all, o_part, o_both, o_send, o_recv,
+    g_own_part, g_all, w_all, o_part, o_sides, o_both0, o_both1, o_send, o_recv,
     in_sems, v_sems, a_sems, p1_sems, p2_sems, p3_sems, p4_sems,
     g1_sems, g2_sems, g3_sems, g4_sems, g5_sems, g6_sems, g7_sems,
-    w1_sems, w2_sems, oc_sems, o_sems,
+    w1_sems, w2_sems, oc_sems, o_sems, known_sems,
 ):
     row = lax.axis_index("row")
     col = lax.axis_index("col")
@@ -86,42 +88,48 @@
     other_core = (row, y * 4 + x_low * 2 + 1 - core)
 
     barrier = pltpu.get_barrier_semaphore()
-    peers = col_peers + far_x + [peer for _, _, peer in z_peers]
+    near_z = [device((z + d) % ZN, x, y, core) for d in (1, ZN - 1)]
+    peers = col_peers + far_x + near_z
     for peer in peers:
         pl.semaphore_signal(barrier, inc=1, device_id=peer, device_id_type=MESH)
+
+    def tell(step):
+        for d in (1 << step, ZN - (1 << step)):
+            where = device((z + d) % ZN, x, y, core)
+            pl.semaphore_signal(known_sems.at[step], inc=1, device_id=where, device_id_type=MESH)
+
+    def hear(step):
+        pl.semaphore_wait(known_sems.at[step], 2)
 
     inputs = [
         pltpu.make_async_copy(src, dst, in_sems.at[i])
         for i, (src, dst) in enumerate(
-            ((a_hbm, a_ref), (v_hbm, v_ref), (f_hbm, f_ref), (order_hbm, order_ref))
+            ((v_hbm, v_ref), (a_hbm, a_ref), (f_hbm, f_ref), (order_hbm, order_ref))
         )
     ]
     for copy in inputs:
         copy.start()
 
     inputs[0].wait()
+    pl.semaphore_wait(barrier, len(peers))
+    tell(0)
+    v_copy = send(v_ref, v_other, v_sems, 0, other_core)
+    sent.append(v_copy)
+    inputs[1].wait()
     a_value = a_ref[...]
     gap = jnp.zeros((ROWS, NB - SHARD), F32)
     for s in range(8):
-        first = a_value[:, s * 400 : s * 400 + 200]
-        second = a_value[:, s * 400 + 200 : s * 400 + 400]
-        a_send[s] = jnp.concatenate([first, gap, second, gap], axis=1)
+        first, second = s * 2 * SHARD, (s * 2 + 1) * SHARD
+        pieces = [
+            a_value[:, first : first + HALF],
+            a_value[:, second : second + HALF],
+            a_value[:, first + HALF : first + SHARD],
+            gap,
+            a_value[:, second + HALF : second + SHARD],
+            gap,
+        ]
+        a_send[s] = jnp.concatenate(pieces, axis=1)
     a_recv[chip] = a_send[chip]
-    inputs[1].wait()
-    for b in range(BLOCKS):
-        up, low = split_parts(padded(v_ref[b]))
-        v_up[b, core] = up
-        v_low[b, core] = low
-    inputs[2].wait()
-    for b in range(BLOCKS):
-        up, low = split_parts(f_ref[b])
-        f_up[b] = up
-        f_low[b] = low
-    inputs[3].wait()
-
-    pl.semaphore_wait(barrier, len(peers))
-    v_copy = send(v_ref, v_other, v_sems, 0, other_core)
-    sent.append(v_copy)
     a_copies = []
     for i, (gy, gx, gc) in enumerate(group[1:-1:2]):
         a_copies.append(
@@ -129,11 +137,29 @@
         )
     sent += a_copies
 
+    for b in range(BLOCKS):
+        up, low = split_parts(padded(v_ref[b]))
+        v_up[b, :, core] = up
+        v_low[b, :, core] = low
+
+    def own_parts(b):
+        return v_up[b, :, core].reshape(NB, NB), v_low[b, :, core].reshape(NB, NB)
+
+    lefts = (3, 3 - core, 2 - core)
+    rights = (2 - 2 * core, 1 - core, 1 - core)
+    for j in range(PAIRS):
+        g_own_part[j] = split_dot(own_parts(lefts[j]), own_parts(rights[j]), LEFT)
+
+    hear(0)
+    tell(1)
     v_copy.wait_recv()
     for b in range(BLOCKS):
         up, low = split_parts(padded(v_other[b]))
-        v_up[b, 1 - core] = up
-        v_low[b, 1 - core] = low
+        v_up[b, :, 1 - core] = up
+        v_low[b, :, 1 - core] = low
+
+    def other_parts(b):
+        return v_up[b, :, 1 - core].reshape(NB, NB), v_low[b, :, 1 - core].reshape(NB, NB)
 
     def v_parts(b):
         return v_up[b].reshape(2 * NB, NB), v_low[b].reshape(2 * NB, NB)
@@ -218,14 +244,19 @@
         sent.extend(copies)
         return copies
 
-    lefts = (3, 3 - core, 2 - core)
-    rights = (2 - 2 * core, 1 - core, 1 - core)
     for j in range(PAIRS):
-        product = split_dot(v_parts(lefts[j]), v_parts(rights[j]), LEFT)
+        product = g_own_part[j] + split_dot(other_parts(lefts[j]), other_parts(rights[j]), LEFT)
         for half in range(2):
             lanes = product[:, half * 128 : half * 128 + 128]
             g_part[half, j] = lanes.reshape(YN, XN, 16, 128)
     g1 = [start_first(half, g_part, g_in1, g1_sems) for half in range(2)]
+    hear(1)
+    tell(2)
+
+    g2 = []
+    for half in range(2):
+        finish_first(half, g1[half], g_part, g_in1, g_mid)
+        g2.append(start_second(half, g_mid, g_in2, g2_sems))
 
     for copy in a_copies:
         copy.wait_recv()
@@ -237,33 +268,41 @@
             p_part[half, i] = product.reshape(YN, XN, 16, NB)
         p1.append(start_first(half, p_part, p_in1, p1_sems))
 
-    g2 = []
-    for half in range(2):
-        finish_first(half, g1[half], g_part, g_in1, g_mid)
-        g2.append(start_second(half, g_mid, g_in2, g2_sems))
     for half in range(2):
         finish_second(half, g2[half], g_mid, g_in2, g_tiles)
     for t in range(12, ZN):
         g_tiles[t] = jnp.zeros((8, 128), F32)
+    hear(2)
     g3 = start_z(g_tiles, g_in3, g3_sems)
+
+    inputs[2].wait()
+    for b in range(BLOCKS):
+        up, low = split_parts(f_ref[b])
+        f_up[b] = up
+        f_low[b] = low
+    inputs[3].wait()
+
+    @pl.loop(0, 16 * ROWS, unroll=8)
+    def _(k):
+        source = order_ref[k]
+        place_ref[k] = (source >> 5 & 1) * (8 * ROWS) + (source >> 6) * ROWS + (source & 31)
 
     p2 = []
     for half in range(2):
         finish_first(half, p1[half], p_part, p_in1, p_mid)
         p2.append(start_second(half, p_mid, p_in2, p2_sems))
+    finish_z(g3, g_tiles, g_in3, g_own)
+    g4 = start_z_back(g_own, g4_sems)
     for half in range(2):
         finish_second(half, p2[half], p_mid, p_in2, p_tiles)
     p3 = start_z(p_tiles, p_in3, p3_sems)
-
-    finish_z(g3, g_tiles, g_in3, g_own)
-    g4 = start_z_back(g_own, g4_sems)
-    finish_z(p3, p_tiles, p_in3, p_own)
-    p4 = start_z_back(p_own, p4_sems)
 
     g_mine = g_all.at[core]
     for j, block in enumerate(finish_z_back(g4, g_own, PAIRS, 1)):
         g_all[core, j // PAIRS, j % PAIRS, y, x] = block
     g5 = [start_back(half, g_mine, g5_sems) for half in range(2)]
+    finish_z(p3, p_tiles, p_in3, p_own)
+    p4 = start_z_back(p_own, p4_sems)
     g6 = [finish_back(half, g_mine, g5[half], g6_sems) for half in range(2)]
     g7 = []
     for half in range(2):
@@ -305,39 +344,53 @@
             w1.append(start_back(i // 2, w_all, w1_sems))
     w2 = [finish_back(half, w_all, w1[half], w2_sems) for half in range(2)]
 
-    for side in range(2):
-        o_part[side] = a_recv[:, :, side * NB : side * NB + NB].reshape(8 * ROWS, NB)
+    w_blocks = {}
+    o_both = (o_both0, o_both1)
+    for part in range(2):
+        o_part[part] = a_recv[:, :, part * NB : part * NB + NB].reshape(8 * ROWS, NB)
+    oc = []
     for half in range(2):
         for copy in w2[half]:
             copy.wait_recv()
         for i in range(2):
-            b = 3 - 2 * half - i
-            parts = split_parts(w_all[half, i].reshape(8 * ROWS, NB))
-            for side in range(2):
-                o_part[side] -= split_dot(parts, (v_up[b, side], v_low[b, side]), RIGHT)
-    oc = send(o_part.at[1 - core], o_both.at[core], oc_sems, 0, other_core)
-    sent.append(oc)
-    o_both[core] = o_part[core]
-    oc.wait_recv()
+            w_blocks[half, i] = split_parts(w_all[half, i].reshape(8 * ROWS, NB))
+        for part in range(2):
+            value = o_part[part]
+            for i in range(2):
+                b = 3 - 2 * half - i
+                v_block = (v_up[b, part].reshape(NB, NB), v_low[b, part].reshape(NB, NB))
+                value = value - split_dot(w_blocks[half, i], v_block, RIGHT)
+            if half == 0:
+                o_part[part] = value
+            else:
+                for side in range(2):
+                    o_sides[part, side] = value[:, side * HALF : side * HALF + HALF]
+                into = o_both[part].at[pl.ds(core * 8 * ROWS, 8 * ROWS)]
+                oc.append(send(o_sides.at[part, 1 - core], into, oc_sems, part, other_core))
+                o_both[part][pl.ds(core * 8 * ROWS, 8 * ROWS)] = o_sides[part, core]
+    sent += oc
     o_copies = []
-    for i, (ty, tx, tc) in enumerate(group):
-        target = ty * 4 + tx * 2 + tc
-
-        @pl.loop(0, ROWS, unroll=8)
-        def _(k):
-            source = order_ref[target * ROWS + k]
-            plane = source // ROWS % 2
-            place = source // (2 * ROWS) * ROWS + source % ROWS
-            o_send[target, pl.ds(k, 1), :] = o_both[plane, pl.ds(place, 1), :]
-
-        if i < 15:
-            o_copies.append(send(o_send.at[target], o_recv.at[col], o_sems, i, (row, target)))
+    for part in range(2):
+        oc[part].wait_recv()
+        for i, (ty, tx, tc) in enumerate(group):
+            target = ty * 4 + tx * 2 + tc
+
+            @pl.loop(0, ROWS, unroll=16)
+            def _(k):
+                place = place_ref[target * ROWS + k]
+                o_send[part, target, pl.ds(k, 1), :] = o_both[part][pl.ds(place, 1), :]
+
+            if i < 15:
+                src, dst = o_send.at[part, target], o_recv.at[part, col]
+                o_copies.append(send(src, dst, o_sems, part * 15 + i, (row, target)))
     sent += o_copies
-    o_recv[col] = o_send[col]
+    for part in range(2):
+        o_recv[part, col] = o_send[part, col]
     for copy in o_copies:
         copy.wait_recv()
     for c in range(16):
-        out_ref[:, c * SHARD : c * SHARD + SHARD] = o_recv[c][:, :SHARD]
+        out_ref[:, c * SHARD : c * SHARD + HALF] = o_recv[0, c]
+        out_ref[:, c * SHARD + HALF : c * SHARD + SHARD] = o_recv[1, c][:, : SHARD - HALF]
 
     for copy in sent:
         copy.wait_send()
@@ -365,24 +418,26 @@
 def per_device(merged_vectors, deflation, vectors, factors):
     rows = 8 * ROWS
     scratch = [
-        pltpu.SMEM(deflation.shape, jnp.int32), vmem(*merged_vectors.shape),
+        pltpu.SMEM(deflation.shape, jnp.int32), pltpu.SMEM(deflation.shape, jnp.int32),
+        vmem(*merged_vectors.shape),
         vmem(*vectors.shape), vmem(*factors.shape),
         vmem(BLOCKS, SHARD, NB),
-        half_vmem(BLOCKS, 2, NB, NB), half_vmem(BLOCKS, 2, NB, NB),
+        half_vmem(BLOCKS, 2, 2, HALF, NB), half_vmem(BLOCKS, 2, 2, HALF, NB),
         half_vmem(BLOCKS, NB, NB), half_vmem(BLOCKS, NB, NB),
         vmem(8, ROWS, 2 * NB), vmem(8, ROWS, 2 * NB),
         *reduce_bufs(2, NB),
         *reduce_bufs(PAIRS, 128),
+        vmem(PAIRS, NB, NB),
         vmem(2, 2, PAIRS, YN, XN, 16, 128),
         vmem(2, 2, YN, XN, 16, NB),
-        vmem(2, rows, NB), vmem(2, rows, NB),
-        vmem(16, ROWS, NB), vmem(16, ROWS, NB),
+        vmem(2, rows, NB), vmem(2, 2, rows, HALF), vmem(2 * rows, HALF), vmem(2 * rows, HALF),
+        vmem(2, 16, ROWS, HALF), vmem(2, 16, ROWS, HALF),
         pltpu.SemaphoreType.DMA((4,)),
         sems(1), sems(7), sems(6), sems(6), sems(15), sems(15),
         sems(6), sems(6), sems(15), sems(15), sems(6), sems(6), sems(8),
-        sems(6), sems(6), sems(1), sems(15),
+        sems(6), sems(6), sems(2), sems(30), pltpu.SemaphoreType.REGULAR((3,)),
     ]
-    in_place = pl.BlockSpec(memory_space=pl.ANY)
+    in_place = pl.BlockSpec(memory_space=pltpu.HBM)
     return pl.pallas_call(
         kernel,
         out_shape=jax.ShapeDtypeStruct(merged_vectors.shape, F32),

time: 92.6 us -> 85.9 us (0.928)
  Pallas kernels: 90.6 us -> 83.9 us
    pallas_call x1, Pallas kernels: 90.6 us -> 83.9 us  [per_device(): pl.pallas_call(kernel, out_shape=jax.ShapeDtypeStruct(merged_vectors.shap...]
where the time goes in v3:
time: 85.9 us; the launch traced here: 85.7 us
  Pallas kernels  83.9 us (98%)
  local copies, waits for them, and re-layouts  1.78 us (2%)
    pallas_call x1, Pallas kernels, per_device(): pl.pallas_call(kernel, out_shape=jax.ShapeDtypeStruct(merged_vectors.shap...  83.9 us
    unnamed x1, local copies, waits for them, and re-layouts  1.78 us

profile of v3, /device:TPU:1, one launch (start us, length us, event | category | flops | bytes accessed | tf_op | source)
XLA Modules:
  0.0 85.7 jit_solution(3181705317166327605)
XLA Ops:
  0.0 83.9 %back_transform.1 = f32[32,3200]{1,0:T(8,128)} custom-call(s32[512]{0:T(512)} %order_hbm.1, f32[32,3200]{1,0:T(8,128)} %a_hbm.1, f32[4,200,256]{2,1,0:T(8,128)} %v_hbm.1, f32[4,256,256]{2,1,0:T(8,128)} %f_hbm.1), custom_call_target="tpu_custom_call" | custom-call | tf_op jit(solution)/shard_map/back_transform/pallas_call | solution.py:441
  83.9 1.8 %copy.6 = f32[32,3200]{1,0:T(8,128)} copy(f32[32,3200]{1,0:T(8,128)} %back_transform.1) | data formatting | bytes 819200

commit v4 on v3

--- a/solution.py
+++ b/solution.py
@@ -32,21 +32,29 @@
     return dot(a[0], b[0], numbers) + dot(a[0], b[1], numbers) + dot(a[1], b[0], numbers)
 
 
+def split_dot_few(a, b, numbers):
+    rows = a[0].shape[0]
+    both = dot(jnp.concatenate(a, axis=0), b[0], numbers)
+    return both[:rows] + dot(a[0], b[1], numbers) + both[rows:]
+
+
 def device(z, x, y, core):
     return (z * 2 + x // 2, y * 4 + (x % 2) * 2 + core)
 
 
 def send(src, dst, sems, index, where):
-    copy = pltpu.make_async_remote_copy(
+    pltpu.make_async_remote_copy(
         src_ref=src,
         dst_ref=dst,
         send_sem=sems.at[0, index],
         recv_sem=sems.at[1, index],
         device_id=where,
         device_id_type=MESH,
-    )
-    copy.start()
-    return copy
+    ).start()
+
+
+def wait_bytes(like, sem):
+    pltpu.make_async_copy(like, like, sem).wait()
 
 
 def padded(values):
@@ -61,7 +69,7 @@
     a_send, a_recv,
     p_part, p_in1, p_mid, p_in2, p_tiles, p_in3, p_own,
     g_part, g_in1, g_mid, g_in2, g_tiles, g_in3, g_own,
-    g_own_part, g_all, w_all, o_part, o_sides, o_both0, o_both1, o_send, o_recv,
+    g_give, g_keep, g_take, g_all, w_all, o_part, o_sides, o_both0, o_both1, o_send, o_recv,
     in_sems, v_sems, a_sems, p1_sems, p2_sems, p3_sems, p4_sems,
     g1_sems, g2_sems, g3_sems, g4_sems, g5_sems, g6_sems, g7_sems,
     w1_sems, w2_sems, oc_sems, o_sems, known_sems,
@@ -73,6 +81,15 @@
     x = (row % 2) * 2 + x_low
     chip = y * 2 + x_low
     sent = []
+
+    def sending(like, sems, index):
+        sent.append((like, sems.at[0, index]))
+        return like, sems.at[1, index]
+
+    def wait_sent():
+        for like, sem in sent:
+            wait_bytes(like, sem)
+        sent.clear()
 
     y_peers = [(d, (y + d) % YN, device(z, x, (y + d) % YN, core)) for d in (2, 1, 3)]
     x_peers = [(d, (x + d) % XN, device(z, (x + d) % XN, y, core)) for d in (2, 1, 3)]
@@ -111,10 +128,25 @@
         copy.start()
 
     inputs[0].wait()
+    for b in range(BLOCKS):
+        up, low = split_parts(padded(v_ref[b]))
+        v_up[b, :, core] = up
+        v_low[b, :, core] = low
+
+    def own_parts(b):
+        return v_up[b, :, core].reshape(NB, NB), v_low[b, :, core].reshape(NB, NB)
+
+    for to, into in ((1 - core, g_give), (core, g_keep)):
+        lefts = (3, 3 - to, 2 - to)
+        rights = (2 - 2 * to, 1 - to, 1 - to)
+        for j in range(PAIRS):
+            into[j] = split_dot(own_parts(lefts[j]), own_parts(rights[j]), LEFT)
     pl.semaphore_wait(barrier, len(peers))
     tell(0)
-    v_copy = send(v_ref, v_other, v_sems, 0, other_core)
-    sent.append(v_copy)
+    send(g_give, g_take, v_sems, 1, other_core)
+    g_copy = sending(g_take, v_sems, 1)
+    send(v_ref, v_other, v_sems, 0, other_core)
+    v_copy = sending(v_other, v_sems, 0)
     inputs[1].wait()
     a_value = a_ref[...]
     gap = jnp.zeros((ROWS, NB - SHARD), F32)
@@ -130,65 +162,32 @@
         ]
         a_send[s] = jnp.concatenate(pieces, axis=1)
     a_recv[chip] = a_send[chip]
-    a_copies = []
-    for i, (gy, gx, gc) in enumerate(group[1:-1:2]):
-        a_copies.append(
-            send(a_send.at[gy * 2 + gx], a_recv.at[chip], a_sems, i, (row, gy * 4 + gx * 2 + core))
-        )
-    sent += a_copies
-
-    for b in range(BLOCKS):
-        up, low = split_parts(padded(v_ref[b]))
-        v_up[b, :, core] = up
-        v_low[b, :, core] = low
-
-    def own_parts(b):
-        return v_up[b, :, core].reshape(NB, NB), v_low[b, :, core].reshape(NB, NB)
-
-    lefts = (3, 3 - core, 2 - core)
-    rights = (2 - 2 * core, 1 - core, 1 - core)
-    for j in range(PAIRS):
-        g_own_part[j] = split_dot(own_parts(lefts[j]), own_parts(rights[j]), LEFT)
-
-    hear(0)
-    tell(1)
-    v_copy.wait_recv()
-    for b in range(BLOCKS):
-        up, low = split_parts(padded(v_other[b]))
-        v_up[b, :, 1 - core] = up
-        v_low[b, :, 1 - core] = low
-
-    def other_parts(b):
-        return v_up[b, :, 1 - core].reshape(NB, NB), v_low[b, :, 1 - core].reshape(NB, NB)
+    for gy, gx, _ in group[1:-1:2]:
+        where = (row, gy * 4 + gx * 2 + core)
+        send(a_send.at[gy * 2 + gx], a_recv.at[chip], a_sems, 0, where)
+    a_copies = sending(a_recv.at[pl.ds(0, 7)], a_sems, 0)
 
     def v_parts(b):
         return v_up[b].reshape(2 * NB, NB), v_low[b].reshape(2 * NB, NB)
 
     def start_first(half, part, into, sems):
-        copies = []
         for d, place, peer in (y_peers, x_peers)[half]:
             src = part.at[0, :, place] if half == 0 else part.at[1, :, :, place]
-            copies.append(send(src, into.at[half, d - 1], sems, half * 3 + d - 1, peer))
-        sent.extend(copies)
-        return copies
+            send(src, into.at[half, d - 1], sems, half, peer)
+        return sending(into.at[half], sems, half)
 
     def finish_first(half, copies, part, into, mid):
-        for copy in copies:
-            copy.wait_recv()
+        wait_bytes(*copies)
         own = part[0, :, y] if half == 0 else part[1, :, :, x]
         mid[half] = own + into[half, 0] + into[half, 1] + into[half, 2]
 
     def start_second(half, mid, into, sems):
-        copies = []
         for d, place, peer in (x_peers, y_peers)[half]:
-            src = mid.at[half, :, place]
-            copies.append(send(src, into.at[half, d - 1], sems, half * 3 + d - 1, peer))
-        sent.extend(copies)
-        return copies
+            send(mid.at[half, :, place], into.at[half, d - 1], sems, half, peer)
+        return sending(into.at[half], sems, half)
 
     def finish_second(half, copies, mid, into, tiles):
-        for copy in copies:
-            copy.wait_recv()
+        wait_bytes(*copies)
         value = mid[half, :, (x, y)[half]] + into[half, 0] + into[half, 1] + into[half, 2]
         count, lanes = value.shape[0], value.shape[2] // 128
         for t in range(count * 2 * lanes):
@@ -197,25 +196,21 @@
             tiles[half * count * 2 * lanes + t] = piece
 
     def start_z(tiles, into, sems):
-        copies = [
-            send(tiles.at[place], into.at[d - 1], sems, d - 1, peer) for d, place, peer in z_peers
-        ]
-        sent.extend(copies)
-        return copies
+        for d, place, peer in z_peers:
+            send(tiles.at[place], into.at[d - 1], sems, 0, peer)
+        return sending(into, sems, 0)
 
     def finish_z(copies, tiles, into, own):
-        for copy in copies:
-            copy.wait_recv()
+        wait_bytes(*copies)
         own[z] = tiles[z] + jnp.sum(into[...], axis=0)
 
     def start_z_back(own, sems):
-        copies = [send(own.at[z], own.at[z], sems, d - 1, peer) for d, _, peer in z_peers]
-        sent.extend(copies)
-        return copies
+        for _, _, peer in z_peers:
+            send(own.at[z], own.at[z], sems, 0, peer)
+        return sending(own.at[pl.ds(0, ZN - 1)], sems, 0)
 
     def finish_z_back(copies, own, count, lanes):
-        for copy in copies:
-            copy.wait_recv()
+        wait_bytes(*copies)
         blocks = []
         for j in range(2 * count):
             base = j * 2 * lanes
@@ -228,28 +223,31 @@
 
     def start_back(half, whole, sems):
         mine = whole.at[half, :, y, x]
-        copies = [
-            send(mine, mine, sems, half * 3 + d - 1, peer) for d, _, peer in (x_peers, y_peers)[half]
-        ]
-        sent.extend(copies)
-        return copies
+        for _, _, peer in (x_peers, y_peers)[half]:
+            send(mine, mine, sems, half, peer)
+        return sending(whole.at[half, :, 0, pl.ds(0, 3)], sems, half)
 
     def finish_back(half, whole, copies, sems):
-        for copy in copies:
-            copy.wait_recv()
+        wait_bytes(*copies)
         mine = whole.at[0, :, y] if half == 0 else whole.at[1, :, :, x]
-        copies = [
-            send(mine, mine, sems, half * 3 + d - 1, peer) for d, _, peer in (y_peers, x_peers)[half]
-        ]
-        sent.extend(copies)
-        return copies
-
+        for _, _, peer in (y_peers, x_peers)[half]:
+            send(mine, mine, sems, half, peer)
+        return sending(whole.at[half, :, pl.ds(0, 3)], sems, half)
+
+    wait_bytes(*g_copy)
     for j in range(PAIRS):
-        product = g_own_part[j] + split_dot(other_parts(lefts[j]), other_parts(rights[j]), LEFT)
+        product = g_keep[j] + g_take[j]
         for half in range(2):
             lanes = product[:, half * 128 : half * 128 + 128]
             g_part[half, j] = lanes.reshape(YN, XN, 16, 128)
     g1 = [start_first(half, g_part, g_in1, g1_sems) for half in range(2)]
+    hear(0)
+    tell(1)
+    wait_bytes(*v_copy)
+    for b in range(BLOCKS):
+        up, low = split_parts(padded(v_other[b]))
+        v_up[b, :, 1 - core] = up
+        v_low[b, :, 1 - core] = low
     hear(1)
     tell(2)
 
@@ -258,8 +256,7 @@
         finish_first(half, g1[half], g_part, g_in1, g_mid)
         g2.append(start_second(half, g_mid, g_in2, g2_sems))
 
-    for copy in a_copies:
-        copy.wait_recv()
+    wait_bytes(*a_copies)
     a_parts = split_parts(a_recv[...].reshape(8 * ROWS, 2 * NB))
     p1 = []
     for half in range(2):
@@ -306,22 +303,15 @@
     g6 = [finish_back(half, g_mine, g5[half], g6_sems) for half in range(2)]
     g7 = []
     for half in range(2):
-        where = y if half == 0 else x
-        arrived = [(where, None)] + [
-            ((where - d) % 4, copy) for d, copy in zip((2, 1, 3), g6[half])
-        ]
-        for i, (place, copy) in enumerate(arrived):
-            if copy is not None:
-                copy.wait_recv()
-            piece = g_mine.at[0, :, place] if half == 0 else g_mine.at[1, :, :, place]
-            g7.append(send(piece, piece, g7_sems, half * 4 + i, other_core))
-    sent += g7
+        wait_bytes(*g6[half])
+        send(g_mine.at[half], g_mine.at[half], g7_sems, half, other_core)
+        g7.append(sending(g_mine.at[half], g7_sems, half))
 
     proj = finish_z_back(p4, p_own, 2, 2)
     w = [None] * BLOCKS
     w[0] = split_dot(split_parts(proj[0]), (f_up[3], f_low[3]), RIGHT)
     for copy in g7:
-        copy.wait_recv()
+        wait_bytes(*copy)
 
     def g_parts(c, j):
         block = jnp.concatenate(
@@ -350,8 +340,7 @@
         o_part[part] = a_recv[:, :, part * NB : part * NB + NB].reshape(8 * ROWS, NB)
     oc = []
     for half in range(2):
-        for copy in w2[half]:
-            copy.wait_recv()
+        wait_bytes(*w2[half])
         for i in range(2):
             w_blocks[half, i] = split_parts(w_all[half, i].reshape(8 * ROWS, NB))
         for part in range(2):
@@ -366,12 +355,12 @@
                 for side in range(2):
                     o_sides[part, side] = value[:, side * HALF : side * HALF + HALF]
                 into = o_both[part].at[pl.ds(core * 8 * ROWS, 8 * ROWS)]
-                oc.append(send(o_sides.at[part, 1 - core], into, oc_sems, part, other_core))
+                send(o_sides.at[part, 1 - core], into, oc_sems, part, other_core)
+                oc.append(sending(o_sides.at[part, 1 - core], oc_sems, part))
                 o_both[part][pl.ds(core * 8 * ROWS, 8 * ROWS)] = o_sides[part, core]
-    sent += oc
     o_copies = []
     for part in range(2):
-        oc[part].wait_recv()
+        wait_bytes(*oc[part])
         for i, (ty, tx, tc) in enumerate(group):
             target = ty * 4 + tx * 2 + tc
 
@@ -382,18 +371,16 @@
 
             if i < 15:
                 src, dst = o_send.at[part, target], o_recv.at[part, col]
-                o_copies.append(send(src, dst, o_sems, part * 15 + i, (row, target)))
-    sent += o_copies
+                send(src, dst, o_sems, part, (row, target))
+        o_copies.append(sending(o_recv.at[part, pl.ds(0, 15)], o_sems, part))
     for part in range(2):
         o_recv[part, col] = o_send[part, col]
+    wait_sent()
     for copy in o_copies:
-        copy.wait_recv()
+        wait_bytes(*copy)
     for c in range(16):
         out_ref[:, c * SHARD : c * SHARD + HALF] = o_recv[0, c]
         out_ref[:, c * SHARD + HALF : c * SHARD + SHARD] = o_recv[1, c][:, : SHARD - HALF]
-
-    for copy in sent:
-        copy.wait_send()
 
 
 def vmem(*shape):
@@ -427,15 +414,15 @@
         vmem(8, ROWS, 2 * NB), vmem(8, ROWS, 2 * NB),
         *reduce_bufs(2, NB),
         *reduce_bufs(PAIRS, 128),
-        vmem(PAIRS, NB, NB),
+        vmem(PAIRS, NB, NB), vmem(PAIRS, NB, NB), vmem(PAIRS, NB, NB),
         vmem(2, 2, PAIRS, YN, XN, 16, 128),
         vmem(2, 2, YN, XN, 16, NB),
         vmem(2, rows, NB), vmem(2, 2, rows, HALF), vmem(2 * rows, HALF), vmem(2 * rows, HALF),
         vmem(2, 16, ROWS, HALF), vmem(2, 16, ROWS, HALF),
         pltpu.SemaphoreType.DMA((4,)),
-        sems(1), sems(7), sems(6), sems(6), sems(15), sems(15),
-        sems(6), sems(6), sems(15), sems(15), sems(6), sems(6), sems(8),
-        sems(6), sems(6), sems(2), sems(30), pltpu.SemaphoreType.REGULAR((3,)),
+        sems(2), sems(1), sems(2), sems(2), sems(1), sems(1),
+        sems(2), sems(2), sems(1), sems(1), sems(2), sems(2), sems(2),
+        sems(2), sems(2), sems(2), sems(2), pltpu.SemaphoreType.REGULAR((3,)),
     ]
     in_place = pl.BlockSpec(memory_space=pltpu.HBM)
     return pl.pallas_call(

time: 85.9 us -> 83.6 us (0.973)
  Pallas kernels: 83.9 us -> 81.6 us
    pallas_call x1, Pallas kernels: 83.9 us -> 81.6 us  [per_device(): pl.pallas_call(kernel, out_shape=jax.ShapeDtypeStruct(merged_vectors.shap...]
where the time goes in v4:
time: 83.6 us; the launch traced here: 83.4 us
  Pallas kernels  81.6 us (98%)
  local copies, waits for them, and re-layouts  1.78 us (2%)
    pallas_call x1, Pallas kernels, per_device(): pl.pallas_call(kernel, out_shape=jax.ShapeDtypeStruct(merged_vectors.shap...  81.6 us
    unnamed x1, local copies, waits for them, and re-layouts  1.78 us

profile of v4, /device:TPU:1, one launch (start us, length us, event | category | flops | bytes accessed | tf_op | source)
XLA Modules:
  0.0 83.4 jit_solution(18324735616821370634)
XLA Ops:
  0.0 81.6 %back_transform.1 = f32[32,3200]{1,0:T(8,128)} custom-call(s32[512]{0:T(512)} %order_hbm.1, f32[32,3200]{1,0:T(8,128)} %a_hbm.1, f32[4,200,256]{2,1,0:T(8,128)} %v_hbm.1, f32[4,256,256]{2,1,0:T(8,128)} %f_hbm.1), custom_call_target="tpu_custom_call" | custom-call | tf_op jit(solution)/shard_map/back_transform/pallas_call | solution.py:428
  81.6 1.8 %copy.6 = f32[32,3200]{1,0:T(8,128)} copy(f32[32,3200]{1,0:T(8,128)} %back_transform.1) | data formatting | bytes 819200

commit v5 on v4

--- a/solution.py
+++ b/solution.py
@@ -32,12 +32,6 @@
     return dot(a[0], b[0], numbers) + dot(a[0], b[1], numbers) + dot(a[1], b[0], numbers)
 
 
-def split_dot_few(a, b, numbers):
-    rows = a[0].shape[0]
-    both = dot(jnp.concatenate(a, axis=0), b[0], numbers)
-    return both[:rows] + dot(a[0], b[1], numbers) + both[rows:]
-
-
 def device(z, x, y, core):
     return (z * 2 + x // 2, y * 4 + (x % 2) * 2 + core)
 
@@ -69,10 +63,10 @@
     a_send, a_recv,
     p_part, p_in1, p_mid, p_in2, p_tiles, p_in3, p_own,
     g_part, g_in1, g_mid, g_in2, g_tiles, g_in3, g_own,
-    g_give, g_keep, g_take, g_all, w_all, o_part, o_sides, o_both0, o_both1, o_send, o_recv,
+    g_give, g_keep, g_take, g_all, p_all, o_part, o_sides, o_both0, o_both1, o_send, o_recv,
     in_sems, v_sems, a_sems, p1_sems, p2_sems, p3_sems, p4_sems,
     g1_sems, g2_sems, g3_sems, g4_sems, g5_sems, g6_sems, g7_sems,
-    w1_sems, w2_sems, oc_sems, o_sems, known_sems,
+    p5_sems, p6_sems, oc_sems, o_sems, known_sems,
 ):
     row = lax.axis_index("row")
     col = lax.axis_index("col")
@@ -301,17 +295,37 @@
     finish_z(p3, p_tiles, p_in3, p_own)
     p4 = start_z_back(p_own, p4_sems)
     g6 = [finish_back(half, g_mine, g5[half], g6_sems) for half in range(2)]
+
+    for i, block in enumerate(finish_z_back(p4, p_own, 2, 2)):
+        p_all[i // 2, i % 2, y, x] = block
+    p5 = [start_back(half, p_all, p5_sems) for half in range(2)]
     g7 = []
     for half in range(2):
         wait_bytes(*g6[half])
         send(g_mine.at[half], g_mine.at[half], g7_sems, half, other_core)
         g7.append(sending(g_mine.at[half], g7_sems, half))
-
-    proj = finish_z_back(p4, p_own, 2, 2)
-    w = [None] * BLOCKS
-    w[0] = split_dot(split_parts(proj[0]), (f_up[3], f_low[3]), RIGHT)
+    p6 = [finish_back(half, p_all, p5[half], p6_sems) for half in range(2)]
+
+    for part in range(2):
+        o_part[part] = a_recv[:, :, part * NB : part * NB + NB].reshape(8 * ROWS, NB)
+
+    def projected(i):
+        return p_all[i // 2, i % 2].reshape(8 * ROWS, NB)
+
+    def combine(value, i):
+        return split_parts(split_dot(split_parts(value), (f_up[3 - i], f_low[3 - i]), RIGHT))
+
+    def subtract(i, part):
+        v_block = (v_up[3 - i, part].reshape(NB, NB), v_low[3 - i, part].reshape(NB, NB))
+        return o_part[part] - split_dot(w_parts[i], v_block, RIGHT)
+
+    wait_bytes(*p6[0])
+    w_parts = [combine(projected(0), 0)]
+    for part in range(2):
+        o_part[part] = subtract(0, part)
     for copy in g7:
         wait_bytes(*copy)
+    wait_bytes(*p6[1])
 
     def g_parts(c, j):
         block = jnp.concatenate(
@@ -320,44 +334,25 @@
         return split_parts(block)
 
     places = {(0, 1): (0, 0), (0, 2): (0, 1), (1, 2): (0, 2), (0, 3): (1, 0), (1, 3): (1, 1), (2, 3): (1, 2)}
-    w_parts = [split_parts(w[0])]
-    w_all[0, 0, y, x] = w[0]
-    w1 = []
     for i in range(1, BLOCKS):
-        value = proj[i]
+        value = projected(i)
         for k in range(i):
             value = value - split_dot(w_parts[k], g_parts(*places[k, i]), PLAIN)
-        value = split_dot(split_parts(value), (f_up[3 - i], f_low[3 - i]), RIGHT)
-        w_parts.append(split_parts(value))
-        w_all[i // 2, i % 2, y, x] = value
-        if i % 2 == 1:
-            w1.append(start_back(i // 2, w_all, w1_sems))
-    w2 = [finish_back(half, w_all, w1[half], w2_sems) for half in range(2)]
-
-    w_blocks = {}
+        w_parts.append(combine(value, i))
+        if i < BLOCKS - 1:
+            for part in range(2):
+                o_part[part] = subtract(i, part)
+
     o_both = (o_both0, o_both1)
+    oc = []
     for part in range(2):
-        o_part[part] = a_recv[:, :, part * NB : part * NB + NB].reshape(8 * ROWS, NB)
-    oc = []
-    for half in range(2):
-        wait_bytes(*w2[half])
-        for i in range(2):
-            w_blocks[half, i] = split_parts(w_all[half, i].reshape(8 * ROWS, NB))
-        for part in range(2):
-            value = o_part[part]
-            for i in range(2):
-                b = 3 - 2 * half - i
-                v_block = (v_up[b, part].reshape(NB, NB), v_low[b, part].reshape(NB, NB))
-                value = value - split_dot(w_blocks[half, i], v_block, RIGHT)
-            if half == 0:
-                o_part[part] = value
-            else:
-                for side in range(2):
-                    o_sides[part, side] = value[:, side * HALF : side * HALF + HALF]
-                into = o_both[part].at[pl.ds(core * 8 * ROWS, 8 * ROWS)]
-                send(o_sides.at[part, 1 - core], into, oc_sems, part, other_core)
-                oc.append(sending(o_sides.at[part, 1 - core], oc_sems, part))
-                o_both[part][pl.ds(core * 8 * ROWS, 8 * ROWS)] = o_sides[part, core]
+        value = subtract(BLOCKS - 1, part)
+        for side in range(2):
+            o_sides[part, side] = value[:, side * HALF : side * HALF + HALF]
+        into = o_both[part].at[pl.ds(core * 8 * ROWS, 8 * ROWS)]
+        send(o_sides.at[part, 1 - core], into, oc_sems, part, other_core)
+        oc.append(sending(o_sides.at[part, 1 - core], oc_sems, part))
+        o_both[part][pl.ds(core * 8 * ROWS, 8 * ROWS)] = o_sides[part, core]
     o_copies = []
     for part in range(2):
         wait_bytes(*oc[part])

time: 83.6 us -> 82.4 us (0.986)
  Pallas kernels: 81.6 us -> 80.4 us
    pallas_call x1, Pallas kernels: 81.6 us -> 80.4 us  [per_device(): pl.pallas_call(kernel, out_shape=jax.ShapeDtypeStruct(merged_vectors.shap...]
where the time goes in v5:
time: 82.4 us; the launch traced here: 82.2 us
  Pallas kernels  80.4 us (98%)
  local copies, waits for them, and re-layouts  1.78 us (2%)
    pallas_call x1, Pallas kernels, per_device(): pl.pallas_call(kernel, out_shape=jax.ShapeDtypeStruct(merged_vectors.shap...  80.4 us
    unnamed x1, local copies, waits for them, and re-layouts  1.78 us

profile of v5, /device:TPU:1, one launch (start us, length us, event | category | flops | bytes accessed | tf_op | source)
XLA Modules:
  0.0 82.2 jit_solution(10769011386520467930)
XLA Ops:
  0.0 80.4 %back_transform.1 = f32[32,3200]{1,0:T(8,128)} custom-call(s32[512]{0:T(512)} %order_hbm.1, f32[32,3200]{1,0:T(8,128)} %a_hbm.1, f32[4,200,256]{2,1,0:T(8,128)} %v_hbm.1, f32[4,256,256]{2,1,0:T(8,128)} %f_hbm.1), custom_call_target="tpu_custom_call" | custom-call | tf_op jit(solution)/shard_map/back_transform/pallas_call | solution.py:423
  80.5 1.8 %copy.6 = f32[32,3200]{1,0:T(8,128)} copy(f32[32,3200]{1,0:T(8,128)} %back_transform.1) | data formatting | bytes 819200

commit v6 on v5

--- a/solution.py
+++ b/solution.py
@@ -427,7 +427,7 @@
         out_specs=pl.BlockSpec(memory_space=pltpu.VMEM),
         scratch_shapes=scratch,
         compiler_params=pltpu.CompilerParams(
-            collective_id=0, has_side_effects=True, vmem_limit_bytes=56 * 1024 * 1024
+            collective_id=0, has_side_effects=True, vmem_limit_bytes=427 * 128 * 1024
         ),
         name="back_transform",
     )(deflation, merged_vectors, vectors, factors)

time: 82.4 us -> 81.3 us (0.987)
    unnamed x1 -> x3, local copies, waits for them, and re-layouts: 1.78 us -> 1.44 us
where the time goes in v6:
time: 81.3 us; the launch traced here: 81.2 us
  Pallas kernels  79.7 us (98%)
  local copies, waits for them, and re-layouts  1.44 us (2%)
    pallas_call x1, Pallas kernels, per_device(): pl.pallas_call(kernel, out_shape=jax.ShapeDtypeStruct(merged_vectors.shap...  79.7 us

profile of v6, /device:TPU:1, one launch (start us, length us, event | category | flops | bytes accessed | tf_op | source)
XLA Modules:
  0.0 81.2 jit_solution(4236360433817727894)
XLA Ops:
  0.0 0.0 copy-start
  0.0 0.7 copy-done
  0.7 79.7 %back_transform.1 = f32[32,3200]{1,0:T(8,128)S(1)} custom-call(s32[512]{0:T(512)S(1)} %copy-done, f32[32,3200]{1,0:T(8,128)} %a_hbm.1, f32[4,200,256]{2,1,0:T(8,128)} %v_hbm.1, f32[4,256,256]{2,1,0:T(8,128)} %f_hbm.1), custom_call_target="tpu_custom_call" | custom-call | tf_op jit(solution)/shard_map/back_transform/pallas_call | solution.py:423
  80.4 0.8 copy.6
Async XLA Ops:
  0.0 0.7 copy-start

commit v7 on v6

--- a/solution.py
+++ b/solution.py
@@ -139,8 +139,6 @@
     tell(0)
     send(g_give, g_take, v_sems, 1, other_core)
     g_copy = sending(g_take, v_sems, 1)
-    send(v_ref, v_other, v_sems, 0, other_core)
-    v_copy = sending(v_other, v_sems, 0)
     inputs[1].wait()
     a_value = a_ref[...]
     gap = jnp.zeros((ROWS, NB - SHARD), F32)
@@ -229,6 +227,8 @@
         return sending(whole.at[half, :, pl.ds(0, 3)], sems, half)
 
     wait_bytes(*g_copy)
+    send(v_ref, v_other, v_sems, 0, other_core)
+    v_copy = sending(v_other, v_sems, 0)
     for j in range(PAIRS):
         product = g_keep[j] + g_take[j]
         for half in range(2):

time: 81.3 us -> 81.4 us (level)
  no operation moved by 1% of the time
where the time goes in v7:
time: 81.4 us; the launch traced here: 81.3 us
  Pallas kernels  79.8 us (98%)
  local copies, waits for them, and re-layouts  1.44 us (2%)
    pallas_call x1, Pallas kernels, per_device(): pl.pallas_call(kernel, out_shape=jax.ShapeDtypeStruct(merged_vectors.shap...  79.8 us

profile of v7, /device:TPU:1, one launch (start us, length us, event | category | flops | bytes accessed | tf_op | source)
XLA Modules:
  0.0 81.3 jit_solution(11083307450043088097)
XLA Ops:
  0.0 0.0 copy-start
  0.0 0.7 copy-done
  0.7 79.8 %back_transform.1 = f32[32,3200]{1,0:T(8,128)S(1)} custom-call(s32[512]{0:T(512)S(1)} %copy-done, f32[32,3200]{1,0:T(8,128)} %a_hbm.1, f32[4,200,256]{2,1,0:T(8,128)} %v_hbm.1, f32[4,256,256]{2,1,0:T(8,128)} %f_hbm.1), custom_call_target="tpu_custom_call" | custom-call | tf_op jit(solution)/shard_map/back_transform/pallas_call | solution.py:423
  80.5 0.8 copy.6
Async XLA Ops:
  0.0 0.7 copy-start
